TPU v7x, 128 devices: a whole 4x4x4 slice. The times are simulated.
128 devices in a mesh: segment: 4 (over z), tok: 32 (over y, x, core).
Axes of the slice: x: 4, y: 4, z: 4, core: 2. Of those that a mesh axis runs over, the one named last changes fastest.
Arguments:
- acts: bfloat16 [4, 4096, 8192], P('segment', 'tok'), may hold values from -6 to 6
- output_gradient: bfloat16 [4, 4096, 1024], P('segment', 'tok'), may hold values from -6 to 6
- frozen: bfloat16 [4, 8192, 1024], P('segment', 'tok'), may hold values from -0.0625 to 0.0625
- adapter_down: bfloat16 [4, 128, 64, 8192], P('segment', 'tok'), may hold values from -0.0625 to 0.0625
- adapter_up: bfloat16 [4, 128, 64, 1024], P('segment', 'tok'), may hold values from -0.1875 to 0.1875
- assign: int32 [4, 4096], P('segment', 'tok'), may hold values from 0 to 127, as said below
- adapter_slot: int32 [128], replicated, may hold values from 0 to 127, as said below
Outputs:
- passed: bfloat16 [4, 4096, 8192], P('segment', 'tok')
- down_gradient: float32 [4, 128, 64, 8192], P('segment', 'tok')
- up_gradient: float32 [4, 128, 64, 1024], P('segment', 'tok')
Inputs may be any that keep to these rules, and one draw needn't show every extreme that they name: A permutation of the slots: adapter a is held in slot adapter_slot[a], on device adapter_slot[a] // 4 of tok. `assign`: the 128 tokens of one device are sorted by adapter. Of one device's tokens at most 10 have adapters held by any one device of tok; in every section some device of tok holds the adapters of exactly 10 tokens of every device.
All inputs are finite; a program needn't handle non-finite values.
Results may differ from a plain program's by a relative error of at most 0.012.
Values may be sent and summed in bfloat16 or wider, within the bound.
A program may use at most 128 MiB of HBM per device.

v0:
```python
import jax
import jax.numpy as jnp
from jax import lax
from jax.sharding import PartitionSpec as P

adapter_scale = 2.0


def passed_along(value, axis, steps):
    count = lax.axis_size(axis)
    pairs = [(source, (source + steps) % count) for source in range(count)]
    return lax.ppermute(value, axis, pairs)


def on_device(acts, output_gradient, frozen, adapter_down, adapter_up, assign, adapter_slot):
    tok_rows = acts.shape[1]
    hidden_width = acts.shape[2]
    output_width = output_gradient.shape[2]
    owner_ranks = lax.axis_size("tok")
    owner_share = adapter_down.shape[1]
    adapter_rank_size = adapter_down.shape[2]
    slot_capacity = max(2, 5 * tok_rows // (2 * owner_ranks))
    inputs = acts[0]
    out_grads = output_gradient[0]
    assigned = assign[0]
    match_table = assigned[:, None] == jnp.arange(adapter_slot.shape[0], dtype=jnp.int32)[None, :]
    slot_position = jnp.sum(jnp.where(match_table, adapter_slot[None, :], 0), axis=1)
    owner_of = slot_position // owner_share
    local_slot = slot_position % owner_share
    owner_hot = (owner_of[:, None] == jnp.arange(owner_ranks, dtype=jnp.int32)[None, :]).astype(
        jnp.int32
    )
    position = jnp.sum(jnp.cumsum(owner_hot, axis=0) * owner_hot, axis=1) - 1
    target_owner = owner_of * slot_capacity + position
    slot_row_list = owner_ranks * slot_capacity
    send_rows = jnp.zeros((slot_row_list, hidden_width), jnp.bfloat16).at[target_owner].set(inputs)
    send_grads = (
        jnp.zeros((slot_row_list, output_width), jnp.bfloat16).at[target_owner].set(out_grads)
    )
    slot_marks = (local_slot[:, None] == jnp.arange(owner_share, dtype=jnp.int32)[None, :]).astype(
        jnp.bfloat16
    )
    send_marks = (
        jnp.zeros((slot_row_list, owner_share), jnp.bfloat16).at[target_owner].set(slot_marks)
    )
    recv_rows, recv_grads, received_marks = (
        lax.all_to_all(
            send_rows.reshape(owner_ranks, slot_capacity, hidden_width),
            "tok",
            split_axis=0,
            concat_axis=0,
            tiled=True,
        ),
        lax.all_to_all(
            send_grads.reshape(owner_ranks, slot_capacity, output_width),
            "tok",
            split_axis=0,
            concat_axis=0,
            tiled=True,
        ),
        lax.all_to_all(
            send_marks.reshape(owner_ranks, slot_capacity, owner_share),
            "tok",
            split_axis=0,
            concat_axis=0,
            tiled=True,
        ),
    )
    recv_rows = recv_rows.reshape(slot_row_list, hidden_width)
    recv_grads = recv_grads.reshape(slot_row_list, output_width)
    column_filter_mask = jnp.repeat(
        received_marks.reshape(slot_row_list, owner_share).astype(jnp.float32),
        adapter_rank_size,
        axis=1,
    )
    stacked_down = adapter_down[0].reshape(owner_share * adapter_rank_size, hidden_width)
    stacked_up = adapter_up[0].reshape(owner_share * adapter_rank_size, output_width)
    low_all = lax.dot_general(
        recv_rows, stacked_down, (((1,), (1,)), ((), ())), preferred_element_type=jnp.float32
    )
    low_kept = (low_all * column_filter_mask).astype(jnp.bfloat16)
    projected_rows = lax.dot_general(
        recv_grads, stacked_up, (((1,), (1,)), ((), ())), preferred_element_type=jnp.float32
    )
    lifted_rows = (adapter_scale * projected_rows * column_filter_mask).astype(jnp.bfloat16)
    down_matrix_gradient = lax.dot_general(
        lifted_rows, recv_rows, (((0,), (0,)), ((), ())), preferred_element_type=jnp.float32
    )
    up_matrix_gradient = adapter_scale * lax.dot_general(
        low_kept, recv_grads, (((0,), (0,)), ((), ())), preferred_element_type=jnp.float32
    )
    adapter_rows = jnp.dot(lifted_rows, stacked_down, preferred_element_type=jnp.float32).astype(
        jnp.bfloat16
    )
    returned_rows = lax.all_to_all(
        adapter_rows.reshape(owner_ranks, slot_capacity, hidden_width),
        "tok",
        split_axis=0,
        concat_axis=0,
        tiled=True,
    )
    adapter_piece = returned_rows.reshape(slot_row_list, hidden_width)[target_owner]
    frozen_piece = lax.dot_general(
        out_grads,
        lax.all_gather(frozen, "tok", axis=1, tiled=True)[0],
        (((1,), (1,)), ((), ())),
        preferred_element_type=jnp.float32,
    ).astype(jnp.bfloat16)
    summed_rows = (frozen_piece.astype(jnp.float32) + adapter_piece.astype(jnp.float32)).astype(
        jnp.bfloat16
    )
    passed = passed_along(summed_rows[None], "segment", -1)
    down_gradient = down_matrix_gradient.reshape(1, owner_share, adapter_rank_size, hidden_width)
    up_gradient = up_matrix_gradient.reshape(1, owner_share, adapter_rank_size, output_width)
    return (passed, down_gradient, up_gradient)


def solution(mesh):
    in_specs = (
        P("segment", "tok", None),
        P("segment", "tok", None),
        P("segment", "tok", None),
        P("segment", "tok", None, None),
        P("segment", "tok", None, None),
        P("segment", "tok"),
        P(),
    )
    out_specs = (
        P("segment", "tok", None),
        P("segment", "tok", None, None),
        P("segment", "tok", None, None),
    )
    return jax.shard_map(
        on_device, mesh=mesh, in_specs=in_specs, out_specs=out_specs, check_vma=False
    )
```

profile of v0, /device:TPU:1, one launch (start us, length us, event | category | flops | bytes accessed | tf_op | source)
XLA Modules:
  0.0 342.4 jit_solution(5558575815736206291)
XLA Ops:
  7.2 0.0 copy-start
  7.2 0.0 all-gather.2.cloned.1.call-start
  7.2 0.7 all-gather.2.cloned.1.call-update
  7.9 0.8 select_reduce_fusion.1
  8.8 0.1 fusion.27
  8.9 0.2 reduce_window_sum.11
  9.0 0.2 select_reduce_fusion
  9.2 1.0 scatter_custom_fusion.1
  10.2 0.1 copy.29
  10.3 0.1 reshape.135
  10.5 0.6 copy.30
  11.1 8.6 %all-to-all-start.1 = ((bf16[32,10,4]{1,2,0:T(4,128)(2,1)}), bf16[32,10,4]{1,2,0:T(4,128)(2,1)S(1)}, u32[]{:S(2)}, u32[]{:S(2)}) async-start(bf16[32,10,4]{1,2,0:T(4,128)(2,1)} %copy.30), calls=%async_computation.1 | async-start | bytes 65536 | tf_op jit(solution)/shard_map/all_to_all | solution.py:61
  19.7 1.8 scatter_custom_fusion
  21.5 1.2 reshape.133
  22.7 4.3 %all-to-all-done.1 = bf16[32,10,4]{1,2,0:T(4,128)(2,1)S(1)} async-done(((bf16[32,10,4]{1,2,0:T(4,128)(2,1)}), bf16[32,10,4]{1,2,0:T(4,128)(2,1)S(1)}, u32[]{:S(2)}, u32[]{:S(2)}) %all-to-all-start.1) | async-done | bytes 2592 | tf_op jit(solution)/shard_map/all_to_all | solution.py:61
  26.9 4.0 %all-to-all-start = ((bf16[32,10,1024]{2,1,0:T(8,128)(2,1)}), bf16[32,10,1024]{2,1,0:T(8,128)(2,1)S(1)}, u32[]{:S(2)}, u32[]{:S(2)}) async-start(bf16[32,10,1024]{2,1,0:T(8,128)(2,1)} %reshape.133), calls=%async_computation | async-start | bytes 2097152 | tf_op jit(solution)/shard_map/all_to_all | solution.py:54
  30.9 0.1 copy.31
  31.0 0.1 copy.32
  31.2 0.1 reshape.143
  31.3 0.9 copy.33
  32.2 17.8 %all-to-all-done = bf16[32,10,1024]{2,1,0:T(8,128)(2,1)S(1)} async-done(((bf16[32,10,1024]{2,1,0:T(8,128)(2,1)}), bf16[32,10,1024]{2,1,0:T(8,128)(2,1)S(1)}, u32[]{:S(2)}, u32[]{:S(2)}) %all-to-all-start) | async-done | bytes 655392 | tf_op jit(solution)/shard_map/all_to_all | solution.py:54
  50.0 1.1 reshape.134
  51.0 1.7 fusion.21
  52.7 6.8 %convolution_convert_fusion = bf16[320,8192]{1,0:T(8,128)(2,1)} fusion(bf16[320,256]{1,0:T(8,128)(2,1)S(1)} %fusion.21, bf16[256,8192]{1,0:T(8,128)(2,1)} %bitcast.61), kind=kOutput, calls=%fused_computation.7 | convolution fusion | flops 1344798720 | bytes 9601024 | tf_op jit(solution)/shard_map/dot_general | solution.py:92
  59.6 8.4 %reshape.137 = bf16[32,10,8192]{2,1,0:T(8,128)(2,1)} reshape(bf16[320,8192]{1,0:T(8,128)(2,1)} %convolution_convert_fusion) | data formatting | bytes 10485760 | tf_op jit(solution)/shard_map/reshape | solution.py:96
  68.0 4.9 %all-to-all-start.2 = ((bf16[32,10,8192]{2,1,0:T(8,128)(2,1)}), bf16[32,10,8192]{2,1,0:T(8,128)(2,1)}, u32[]{:S(2)}, u32[]{:S(2)}) async-start(bf16[32,10,8192]{2,1,0:T(8,128)(2,1)} %reshape.137), calls=%async_computation.2 | async-start | bytes 16777216 | tf_op jit(solution)/shard_map/all_to_all | solution.py:95
  73.0 0.0 copy-done
  73.0 6.5 %scatter_custom_fusion.2 = bf16[320,8192]{1,0:T(8,128)(2,1)} fusion(s32[128]{0:T(128)S(1)} %fusion.33, bf16[]{:T(256)} %constant.37.clone.1, bf16[1,128,8192]{2,1,0:T(8,128)(2,1)S(1)} %copy-done), kind=kCustom, calls=%fused_computation.13 | custom fusion | bytes 7340034 | tf_op jit(solution)/shard_map/scatter | solution.py:36
  79.5 8.4 %reshape.140 = bf16[32,10,8192]{2,1,0:T(8,128)(2,1)} reshape(bf16[320,8192]{1,0:T(8,128)(2,1)} %scatter_custom_fusion.2) | data formatting | bytes 10485760 | tf_op jit(solution)/shard_map/reshape | solution.py:48
  87.8 99.8 %all-to-all-done.2 = bf16[32,10,8192]{2,1,0:T(8,128)(2,1)} async-done(((bf16[32,10,8192]{2,1,0:T(8,128)(2,1)}), bf16[32,10,8192]{2,1,0:T(8,128)(2,1)}, u32[]{:S(2)}, u32[]{:S(2)}) %all-to-all-start.2) | async-done | bytes 5242912 | tf_op jit(solution)/shard_map/all_to_all | solution.py:95
  187.6 12.0 %all-to-all-start.3 = ((bf16[32,10,8192]{2,1,0:T(8,128)(2,1)}), bf16[32,10,8192]{2,1,0:T(8,128)(2,1)}, u32[]{:S(2)}, u32[]{:S(2)}) async-start(bf16[32,10,8192]{2,1,0:T(8,128)(2,1)} %reshape.140), calls=%async_computation.3 | async-start | bytes 16777216 | tf_op jit(solution)/shard_map/all_to_all | solution.py:47
  199.6 8.7 %reshape.138 = bf16[320,8192]{1,0:T(8,128)(2,1)} reshape(bf16[32,10,8192]{2,1,0:T(8,128)(2,1)} %all-to-all-done.2) | data formatting | bytes 10485760 | tf_op jit(solution)/shard_map/reshape | solution.py:102
  208.3 0.0 copy-start.3
  208.3 7.0 %gather_fusion = bf16[128,8192]{1,0:T(8,128)(2,1)S(1)} fusion(bf16[320,8192]{1,0:T(8,128)(2,1)} %reshape.138, s32[1024]{0:T(1024)S(1)} %pad_clamp_fusion), kind=kCustom, calls=%fused_computation | custom fusion | bytes 4194816 | tf_op jit(solution)/shard_map/gather | solution.py:102
  215.3 0.0 all-gather.2.cloned.1.call-done
  215.3 0.0 copy-done.3
  215.3 12.7 %fusion.14 = bf16[1,128,8192]{2,1,0:T(8,128)(2,1)} fusion(bf16[1,8192,1024]{2,1,0:T(8,128)(2,1)} %all-gather.2.cloned.1.call-done, bf16[128,8192]{1,0:T(8,128)(2,1)S(1)} %gather_fusion, bf16[1,128,1024]{2,1,0:T(8,128)(2,1)S(1)} %copy-done.3), kind=kOutput, calls=%fused_computation.12 | convolution fusion | flops 2152726528 | bytes 21233664 | tf_op jit(solution)/shard_map/dot_general | solution.py:103
  228.0 2.7 collective-permute-start
  230.8 0.2 copy.34
  230.9 68.5 %all-to-all-done.3 = bf16[32,10,8192]{2,1,0:T(8,128)(2,1)} async-done(((bf16[32,10,8192]{2,1,0:T(8,128)(2,1)}), bf16[32,10,8192]{2,1,0:T(8,128)(2,1)}, u32[]{:S(2)}, u32[]{:S(2)}) %all-to-all-start.3) | async-done | bytes 5242912 | tf_op jit(solution)/shard_map/all_to_all | solution.py:47
  299.4 8.7 %reshape.176 = bf16[320,8192,1]{1,0,2:T(8,128)(2,1)} reshape(bf16[32,10,8192]{2,1,0:T(8,128)(2,1)} %all-to-all-done.3) | data formatting | bytes 10485760 | tf_op jit(solution)/shard_map/reshape | solution.py:69
  308.1 8.7 %reshape.141 = bf16[320,8192]{1,0:T(8,128)(2,1)} reshape(bf16[32,10,8192]{2,1,0:T(8,128)(2,1)} %all-to-all-done.3) | data formatting | bytes 10485760 | tf_op jit(solution)/shard_map/reshape | solution.py:69
  316.8 0.0 copy-start.2
  316.8 0.0 copy-start.4
  316.8 0.0 copy-start.1
  316.8 8.4 %convolution_bitcast_fusion = f32[1,4,64,8192]{3,2,1,0:T(8,128)} fusion(bf16[4,64,320]{2,1,0:T(8,128)(2,1)S(1)} %bitcast.65, bf16[320,8192,1]{1,0,2:T(8,128)(2,1)} %reshape.176), kind=kOutput, calls=%fused_computation.6 | convolution fusion | flops 1342177280 | bytes 13795328 | tf_op jit(solution)/shard_map/dot_general | solution.py:86
  325.2 0.0 copy-done.2
  325.2 0.0 copy-done.4
  325.2 7.3 %convolution_multiply_fusion = f32[256,1024]{1,0:T(8,128)} fusion(bf16[320,1024]{1,0:T(8,128)(2,1)S(1)} %copy-done.2, f32[320,256]{1,0:T(8,128)S(1)} %copy-done.4, bf16[320,8192]{1,0:T(8,128)(2,1)} %reshape.141, bf16[256,8192]{1,0:T(8,128)(2,1)} %bitcast.62), kind=kOutput, calls=%fused_computation.16 | convolution fusion | flops 1510375424 | bytes 11468800 | tf_op jit(solution)/shard_map/dot_general | solution.py:89
  332.5 0.0 collective-permute-done
  332.5 3.1 copy.37
  335.6 0.0 copy-done.1
  (4 shorter events, 0.1 us)
Async XLA Ops:
  7.2 65.8 %copy-start = (bf16[1,128,8192]{2,1,0:T(8,128)(2,1)S(1)}, bf16[1,128,8192]{2,1,0:T(8,128)(2,1)}, u32[]{:S(2)}) copy-start(bf16[1,128,8192]{2,1,0:T(8,128)(2,1)} %param.7) | copy-start | bytes 6291460
  7.2 208.1 %all-gather.2.cloned.1.call-start = ((), (), s32[]{:S(2)}) async-start(), calls=%async_computation.4 | async-start | bytes 17301504 | tf_op jit(solution)/shard_map/all_gather | solution.py:105
  11.1 15.8 %all-to-all-start.1 = ((bf16[32,10,4]{1,2,0:T(4,128)(2,1)}), bf16[32,10,4]{1,2,0:T(4,128)(2,1)S(1)}, u32[]{:S(2)}, u32[]{:S(2)}) async-start(bf16[32,10,4]{1,2,0:T(4,128)(2,1)} %copy.30), calls=%async_computation.1 | async-start | bytes 65536 | tf_op jit(solution)/shard_map/all_to_all | solution.py:61
  26.9 23.0 %all-to-all-start = ((bf16[32,10,1024]{2,1,0:T(8,128)(2,1)}), bf16[32,10,1024]{2,1,0:T(8,128)(2,1)S(1)}, u32[]{:S(2)}, u32[]{:S(2)}) async-start(bf16[32,10,1024]{2,1,0:T(8,128)(2,1)} %reshape.133), calls=%async_computation | async-start | bytes 2097152 | tf_op jit(solution)/shard_map/all_to_all | solution.py:54
  68.0 119.6 %all-to-all-start.2 = ((bf16[32,10,8192]{2,1,0:T(8,128)(2,1)}), bf16[32,10,8192]{2,1,0:T(8,128)(2,1)}, u32[]{:S(2)}, u32[]{:S(2)}) async-start(bf16[32,10,8192]{2,1,0:T(8,128)(2,1)} %reshape.137), calls=%async_computation.2 | async-start | bytes 16777216 | tf_op jit(solution)/shard_map/all_to_all | solution.py:95
  187.6 111.8 %all-to-all-start.3 = ((bf16[32,10,8192]{2,1,0:T(8,128)(2,1)}), bf16[32,10,8192]{2,1,0:T(8,128)(2,1)}, u32[]{:S(2)}, u32[]{:S(2)}) async-start(bf16[32,10,8192]{2,1,0:T(8,128)(2,1)} %reshape.140), calls=%async_computation.3 | async-start | bytes 16777216 | tf_op jit(solution)/shard_map/all_to_all | solution.py:47
  208.3 7.0 %copy-start.3 = (bf16[1,128,1024]{2,1,0:T(8,128)(2,1)S(1)}, bf16[1,128,1024]{2,1,0:T(8,128)(2,1)}, u32[]{:S(2)}) copy-start(bf16[1,128,1024]{2,1,0:T(8,128)(2,1)} %param.8) | copy-start | bytes 786436
  228.0 104.4 %collective-permute-start = (bf16[1,128,8192]{2,1,0:T(8,128)(2,1)}, bf16[1,128,8192]{2,1,0:T(8,128)(2,1)}, u32[]{:S(2)}, u32[]{:S(2)}) collective-permute-start(bf16[1,128,8192]{2,1,0:T(8,128)(2,1)} %fusion.14), channel_id=1, source_target_pairs={{0,96},{32,0},{64,32},{96,64},{1,97},{33,1},{65,33},{97,65},{2,98}... | collective-permute-start | bytes 6291464 | tf_op jit(solution)/shard_map/ppermute | solution.py:12
  316.8 8.4 %copy-start.2 = (bf16[320,1024]{1,0:T(8,128)(2,1)S(1)}, bf16[320,1024]{1,0:T(8,128)(2,1)}, u32[]{:S(2)}) copy-start(bf16[320,1024]{1,0:T(8,128)(2,1)} %reshape.134) | copy-start | bytes 1966084
  316.8 8.4 %copy-start.4 = (f32[320,256]{1,0:T(8,128)S(1)}, f32[320,256]{1,0:T(8,128)}, u32[]{:S(2)}) copy-start(f32[320,256]{1,0:T(8,128)} %copy.33) | copy-start | bytes 983044
  316.8 18.7 %copy-start.1 = (bf16[1,128,8192]{2,1,0:T(8,128)(2,1)S(1)}, bf16[1,128,8192]{2,1,0:T(8,128)(2,1)}, u32[]{:S(2)}) copy-start(bf16[1,128,8192]{2,1,0:T(8,128)(2,1)} %param.7) | copy-start | bytes 6291460
Sparse Core Ops, SparseCore 0:
  10.3 161.4 all-gather.1
where the time goes:
time: 349 us; the launch traced here: 342 us
  waiting for transfers between devices  191 us (55%)
  local copies, waits for them, and re-layouts  65.8 us (19%)
  matrix products  36.9 us (11%)
  starting transfers between devices  32.3 us (9%)
  between operations  14.2 us (4%)
    all_to_all x1, waiting for transfers between devices, on_device(): lax.all_to_all(adapter_rows.reshape(owner_ranks, slot_capacity, hidden_wi...  99.8 us
    all_to_all x1, waiting for transfers between devices, on_device(): lax.all_to_all(send_rows.reshape(owner_ranks, slot_capacity, hidden_width...  68.5 us
    all_to_all x1, waiting for transfers between devices, on_device(): lax.all_to_all(send_grads.reshape(owner_ranks, slot_capacity, output_widt...  17.8 us
    reshape x2, local copies, waits for them, and re-layouts, on_device(): recv_rows = recv_rows.reshape(slot_row_list, hidden_width)  17.4 us
    dot_general x1, matrix products, on_device(): lax.dot_general(out_grads, lax.all_gather(frozen, 'tok', axis=1, tiled=Tr...  12.7 us
    all_to_all x1, starting transfers between devices, on_device(): lax.all_to_all(send_rows.reshape(owner_ranks, slot_capacity, hidden_width...  12 us
    reshape x1, local copies, waits for them, and re-layouts, on_device(): returned_rows.reshape(slot_row_list, hidden_width)[target_owner]  8.69 us
    all_to_all x1, starting transfers between devices, on_device(): lax.all_to_all(send_marks.reshape(owner_ranks, slot_capacity, owner_share...  8.59 us
  transfers between devices with their start and end apart: 6, of which 4 were waited for; matrix products, arithmetic and copies ran while one was open for 30% of the time, Pallas kernels for 0%

commit v1 on v0

v1 whole, which is shorter than its diff:
```python
import functools

import jax
import jax.numpy as jnp
from jax import lax
from jax.experimental import pallas as pl
from jax.experimental.pallas import tpu as pltpu
from jax.sharding import PartitionSpec as P

MESH = pl.DeviceIdType.MESH
BF16 = jnp.bfloat16
F32 = jnp.float32
ADAPTER_SCALE = 2.0

TOKENS = 128
WIDTH = 8192
VALUE = 1024
RANK_ROWS = 256
OWNERS = 32
CAP = 10
SLICES = 8
SLICE = WIDTH // SLICES
PIECE = 16
CHUNKS = SLICES * CAP // PIECE
ROWS = OWNERS * PIECE
TILE = 256
MARK = 128
NX = 4


def slices_of(chunk):
    first, last = chunk * PIECE // CAP, (chunk * PIECE + PIECE - 1) // CAP
    return list(range(first, last + 1))


def first_chunk(j):
    return j * CAP // PIECE


def last_chunk(j):
    return (j * CAP + CAP - 1) // PIECE


def iota(shape, axis):
    return lax.broadcasted_iota(jnp.int32, shape, axis)


def dot(a, b, precision=None):
    return lax.dot_general(a, b, (((1,), (0,)), ((), ())), precision=precision, preferred_element_type=F32)


def dot_t(a, b):
    return lax.dot_general(a, b, (((1,), (1,)), ((), ())), preferred_element_type=F32)


def one_hot(flag):
    return jnp.where(flag, 1.0, 0.0).astype(BF16)


def pick(chunk, j, axis, dest):
    shape = (ROWS, TOKENS) if axis == 0 else (TOKENS, ROWS)
    row = iota(shape, axis)
    rank = (row & 15) + (PIECE * chunk - CAP * j)
    target = (row >> 4) * CAP + rank
    return one_hot((dest == target) & (rank >= 0) & (rank < CAP))


def spread(chunk, js, axis):
    shape = (128, 128)
    row, col = iota(shape, axis), iota(shape, 1 - axis)
    out = None
    for j in js:
        rank = (row & 15) + (PIECE * chunk - CAP * j)
        flag = ((row >> 4) == (col >> 4)) & ((col & 15) == rank) & (rank >= 0) & (rank < CAP)
        out = flag if out is None else out | flag
    return jnp.where(out, 1.0, 0.0)


def kernel(
    acts, grads, frozen, down, up, assign, slots,
    passed, down_grad, up_grad,
    acts_v, grads_v, down_v, up_v, dest_row, dest_col,
    gs, gr, fs, fr, rs, rr, gx, wy, ft, fp,
    lift_src, lift_t, mask_t, lift_q, liftt_q, low_q, low_t, pend, fin, dg, ug,
    in_sem, g_sem, f_send, f_recv, r_send, r_recv, gx_sem, wy_sem, fp_sem, z_send, z_recv, dg_sem, ug_sem,
):
    seg = lax.axis_index("segment")
    me = lax.axis_index("tok")
    y, x, core = me // 8, (me // 2) % 4, me % 2
    col8 = me % 8
    before, after = (seg + 3) % 4, (seg + 1) % 4

    loads = [
        pltpu.make_async_copy(grads, grads_v, in_sem.at[0]),
        pltpu.make_async_copy(acts, acts_v, in_sem.at[1]),
        pltpu.make_async_copy(up, up_v, in_sem.at[2]),
        pltpu.make_async_copy(down, down_v, in_sem.at[3]),
        pltpu.make_async_copy(frozen, wy.at[y], in_sem.at[4]),
        pltpu.make_async_copy(grads, gx.at[col8], in_sem.at[5]),
    ]
    for load in loads:
        load.start()

    barrier = pltpu.get_barrier_semaphore()

    def greet(k, carry):
        pl.semaphore_signal(barrier, inc=1, device_id=(seg, (me + k) % OWNERS), device_id_type=MESH)
        return carry

    lax.fori_loop(1, OWNERS, greet, 0)
    pl.semaphore_signal(barrier, inc=1, device_id=(after, me), device_id_type=MESH)

    match = one_hot(assign[...] == iota((128, 128), 0))
    slot = dot(jnp.broadcast_to(slots[...], (16, 128)).astype(F32).astype(BF16), match)[0:1].astype(jnp.int32)
    owner, local = slot >> 2, slot & 3
    hot = jnp.where(owner == iota((OWNERS, TOKENS), 0), 1.0, 0.0)
    earlier = one_hot(iota((TOKENS, TOKENS), 0) < iota((TOKENS, TOKENS), 1))
    rank = jnp.sum(hot * dot(hot.astype(BF16), earlier), axis=0, keepdims=True)
    dest = owner * CAP + rank.astype(jnp.int32)
    dest_row[...] = jnp.broadcast_to(dest, (8, TOKENS))
    dest_col[...] = jnp.transpose(jnp.broadcast_to(dest.astype(F32), (TOKENS, TOKENS))).astype(jnp.int32)

    local_hot = one_hot(local == iota((MARK, TOKENS), 0))
    row = iota((ROWS, TOKENS), 0)
    chosen = one_hot((dest == (row >> 4) * CAP + (row & 15)) & ((row & 15) < CAP))
    gs[:, VALUE:] = dot_t(chosen, local_hot).astype(BF16)
    loads[0].wait()
    for c0 in range(0, VALUE, TILE):
        gs[:, c0 : c0 + TILE] = dot(chosen, grads_v[:, c0 : c0 + TILE]).astype(BF16)

    def piece(owner_at):
        return pl.ds(pl.multiple_of(owner_at * PIECE, PIECE), PIECE)

    def send_pieces(src, dst, send_sem, recv_sem):
        def one(k, carry):
            to = (me + k) % OWNERS
            pltpu.make_async_remote_copy(
                src_ref=src.at[piece(to)],
                dst_ref=dst.at[piece(me)],
                send_sem=send_sem,
                recv_sem=recv_sem,
                device_id=(seg, to),
                device_id_type=MESH,
            ).start()
            return carry

        lax.fori_loop(1, OWNERS, one, 0)
        dst[piece(me)] = src[piece(me)]

    def wait_pieces(buf, sem):
        others = buf.at[pl.ds(0, ROWS - PIECE)]
        pltpu.make_async_copy(others, others, sem).wait()

    pl.semaphore_wait(barrier, OWNERS)
    send_pieces(gs, gr, g_sem.at[0], g_sem.at[1])

    def send_frozen(k, carry):
        to = ((y + k) % 4) * 8 + col8
        pltpu.make_async_remote_copy(
            src_ref=frozen, dst_ref=wy.at[y], send_sem=wy_sem.at[0], recv_sem=wy_sem.at[1],
            device_id=(seg, to), device_id_type=MESH,
        ).start()
        return carry

    def send_grads(k, carry):
        to = y * 8 + (col8 + k) % 8
        pltpu.make_async_remote_copy(
            src_ref=grads, dst_ref=gx.at[col8], send_sem=gx_sem.at[0], recv_sem=gx_sem.at[1],
            device_id=(seg, to), device_id_type=MESH,
        ).start()
        return carry

    lax.fori_loop(1, 4, send_frozen, 0)
    lax.fori_loop(1, 8, send_grads, 0)

    def send_acts(q):
        src = fs.at[q]

        def step(ct, carry):
            cols = pl.ds(pl.multiple_of(ct * TILE, TILE), TILE)
            total = None
            for j in slices_of(q):
                mine = pl.ds(pl.multiple_of(j * SLICE + ct * TILE, TILE), TILE)
                term = dot(pick(q, j, 0, dest_row[0:1]), acts_v[:, mine])
                total = term if total is None else total + term
            src[:, cols] = total.astype(BF16)
            return carry

        lax.fori_loop(0, SLICE // TILE, step, 0)
        send_pieces(src, fr.at[q], f_send.at[q], f_recv.at[q])

    loads[1].wait()
    send_acts(0)

    loads[2].wait()
    wait_pieces(gr, g_sem.at[1])
    expand = one_hot(iota((RANK_ROWS, MARK), 0) >> 6 == iota((RANK_ROWS, MARK), 1))
    marks = gr[:, VALUE:]
    mask_t[...] = dot_t(expand, marks).astype(BF16)
    lift_src[...] = (ADAPTER_SCALE * dot_t(gr[:, :VALUE], up_v[...]) * dot_t(marks, expand)).astype(BF16)
    lift_t[...] = jnp.transpose(lift_src[...].astype(F32)).astype(BF16)

    loads[3].wait()

    def send_terms(q):
        dst = rs.at[q]
        js = slices_of(q)
        for n, j in enumerate(js):
            move = spread(q, [j], 0).astype(BF16)
            for b in range(0, ROWS, 128):
                lift_q[n, b : b + 128] = dot(move, lift_src[b : b + 128]).astype(BF16)

        def step(ct, carry):
            cols = pl.ds(pl.multiple_of(ct * TILE, TILE), TILE)
            total = None
            for n, j in enumerate(js):
                mine = pl.ds(pl.multiple_of(j * SLICE + ct * TILE, TILE), TILE)
                term = dot(lift_q[n], down_v[:, mine])
                total = term if total is None else total + term
            dst[:, cols] = total.astype(BF16)
            return carry

        lax.fori_loop(0, SLICE // TILE, step, 0)
        send_pieces(dst, rr.at[q], r_send.at[q], r_recv.at[q])

    send_terms(0)
    send_terms(1)

    loads[4].wait()
    loads[5].wait()
    pltpu.make_async_copy(wy.at[pl.ds(0, 3)], wy.at[pl.ds(0, 3)], wy_sem.at[1]).wait()
    pltpu.make_async_copy(gx.at[pl.ds(0, 7)], gx.at[pl.ds(0, 7)], gx_sem.at[1]).wait()

    def frozen_step(k, carry):
        half, yy = k // 4, k % 4
        lhs = gx[pl.ds(half * 4, 4)].reshape(4 * TOKENS, VALUE)
        res = dot_t(lhs, wy[yy]).astype(BF16).reshape(4, TOKENS, 256)
        ft[pl.ds(half * 4, 4), :, pl.ds(pl.multiple_of(yy * 256, 256), 256)] = res
        return carry

    lax.fori_loop(0, 8, frozen_step, 0)
    fp[col8] = ft[col8]

    def send_tiles(k, carry):
        other = (col8 + k) % 8
        pltpu.make_async_remote_copy(
            src_ref=ft.at[other], dst_ref=fp.at[col8], send_sem=fp_sem.at[0], recv_sem=fp_sem.at[1],
            device_id=(seg, y * 8 + other), device_id_type=MESH,
        ).start()
        return carry

    lax.fori_loop(1, 8, send_tiles, 0)

    for q in range(2, CHUNKS):
        send_terms(q)
    for q in range(1, CHUNKS):
        send_acts(q)

    low_t[...] = jnp.zeros_like(low_t)

    def out_copy(j):
        cols = pl.ds(j * SLICE, SLICE)
        return pltpu.make_async_copy(dg.at[j % 4], down_grad.at[:, cols], dg_sem.at[j])

    def take_acts(q):
        js = slices_of(q)
        wait_pieces(fr.at[q], f_recv.at[q])
        for n, j in enumerate(js):
            move = spread(q, [j], 1).astype(BF16)
            for b in range(0, ROWS, 128):
                liftt_q[n, :, b : b + 128] = dot(lift_t[:, b : b + 128], move).astype(BF16)
            if first_chunk(j) == q and j >= 4:
                out_copy(j - 4).wait()
        low_q[...] = jnp.zeros_like(low_q)

        def step(ct, carry):
            cols = pl.ds(pl.multiple_of(ct * TILE, TILE), TILE)
            block = fr[q, :, cols]
            total = low_q[...]
            for n, j in enumerate(js):
                mine = pl.ds(pl.multiple_of(j * SLICE + ct * TILE, TILE), TILE)
                rank_at = (iota((RANK_ROWS, ROWS), 1) & 15) + (PIECE * q - CAP * j)
                total += jnp.where((rank_at >= 0) & (rank_at < CAP), dot_t(down_v[:, mine], block), 0.0)
                term = dot(liftt_q[n], block)
                if first_chunk(j) != q:
                    term += dg[j % 4, :, cols]
                dg[j % 4, :, cols] = term
            low_q[...] = total
            return carry

        lax.fori_loop(0, SLICE // TILE, step, 0)
        back = spread(q, js, 0)
        for b in range(0, ROWS, 128):
            low_t[:, b : b + 128] += dot(low_q[:, b : b + 128], back, lax.Precision.HIGHEST)
        for j in js:
            if last_chunk(j) == q:
                out_copy(j).start()

    def hand_on(j):
        cols = pl.ds(j * SLICE, SLICE)
        return pltpu.make_async_remote_copy(
            src_ref=fin.at[:, cols], dst_ref=passed.at[:, cols], send_sem=z_send.at[j], recv_sem=z_recv.at[j],
            device_id=(before, me), device_id_type=MESH,
        )

    def take_terms(q):
        js = slices_of(q)
        wait_pieces(rr.at[q], r_recv.at[q])

        def step(ct, carry):
            cols = pl.ds(pl.multiple_of(ct * TILE, TILE), TILE)
            block = rr[q, :, cols]
            for j in js:
                dest = jnp.concatenate([dest_col[...]] * (ROWS // 128), axis=1)
                term = dot(pick(q, j, 1, dest), block)
                if first_chunk(j) != q:
                    term += pend[:, cols].astype(F32)
                if last_chunk(j) != q:
                    pend[:, cols] = term.astype(BF16)
                else:
                    part = fp[4 * (j % 2) + ct, :, (j // 2) * 256 : (j // 2) * 256 + 256]
                    mine = pl.ds(pl.multiple_of(j * SLICE + ct * TILE, TILE), TILE)
                    fin[:, mine] = (part.astype(F32) + term.astype(BF16).astype(F32)).astype(BF16)
            return carry

        lax.fori_loop(0, SLICE // TILE, step, 0)
        for j in js:
            if last_chunk(j) == q:
                hand_on(j).start()

    take_acts(0)
    pltpu.make_async_copy(fp.at[pl.ds(0, 7)], fp.at[pl.ds(0, 7)], fp_sem.at[1]).wait()
    for q in range(CHUNKS):
        take_terms(q)
    for q in range(1, CHUNKS):
        take_acts(q)

    low_b = (low_t[...] * mask_t[...].astype(F32)).astype(BF16)
    for c0 in range(0, VALUE, TILE):
        ug[:, c0 : c0 + TILE] = ADAPTER_SCALE * dot(low_b, gr[:, c0 : c0 + TILE])
    up_copy = pltpu.make_async_copy(ug, up_grad, ug_sem.at[0])
    up_copy.start()

    wait_pieces(gs, g_sem.at[0])
    pltpu.make_async_copy(wy.at[pl.ds(0, 3)], wy.at[pl.ds(0, 3)], wy_sem.at[0]).wait()
    pltpu.make_async_copy(gx.at[pl.ds(0, 7)], gx.at[pl.ds(0, 7)], gx_sem.at[0]).wait()
    pltpu.make_async_copy(ft.at[pl.ds(0, 7)], ft.at[pl.ds(0, 7)], fp_sem.at[0]).wait()
    for q in range(CHUNKS):
        wait_pieces(fs.at[q], f_send.at[q])
        wait_pieces(rs.at[q], r_send.at[q])
    for j in range(SLICES):
        hand_on(j).wait()
    for j in range(SLICES - 4, SLICES):
        out_copy(j).wait()
    up_copy.wait()


def on_device(acts, output_gradient, frozen, adapter_down, adapter_up, assign, adapter_slot):
    hbm = pl.BlockSpec(memory_space=pl.ANY)
    vmem = pl.BlockSpec(memory_space=pltpu.VMEM)
    dma = pltpu.SemaphoreType.DMA
    passed, down_grad, up_grad = pl.pallas_call(
        kernel,
        out_shape=(
            jax.ShapeDtypeStruct((TOKENS, WIDTH), BF16),
            jax.ShapeDtypeStruct((RANK_ROWS, WIDTH), F32),
            jax.ShapeDtypeStruct((RANK_ROWS, VALUE), F32),
        ),
        in_specs=[hbm] * 5 + [vmem] * 2,
        out_specs=[hbm] * 3,
        scratch_shapes=[
            pltpu.VMEM((TOKENS, WIDTH), BF16),
            pltpu.VMEM((TOKENS, VALUE), BF16),
            pltpu.VMEM((RANK_ROWS, WIDTH), BF16),
            pltpu.VMEM((RANK_ROWS, VALUE), BF16),
            pltpu.VMEM((8, TOKENS), jnp.int32),
            pltpu.VMEM((TOKENS, TOKENS), jnp.int32),
            pltpu.VMEM((ROWS, VALUE + MARK), BF16),
            pltpu.VMEM((ROWS, VALUE + MARK), BF16),
            pltpu.VMEM((CHUNKS, ROWS, SLICE), BF16),
            pltpu.VMEM((CHUNKS, ROWS, SLICE), BF16),
            pltpu.VMEM((CHUNKS, ROWS, SLICE), BF16),
            pltpu.VMEM((CHUNKS, ROWS, SLICE), BF16),
            pltpu.VMEM((8, TOKENS, VALUE), BF16),
            pltpu.VMEM((4, 256, VALUE), BF16),
            pltpu.VMEM((8, TOKENS, 1024), BF16),
            pltpu.VMEM((8, TOKENS, 1024), BF16),
            pltpu.VMEM((ROWS, RANK_ROWS), BF16),
            pltpu.VMEM((RANK_ROWS, ROWS), BF16),
            pltpu.VMEM((RANK_ROWS, ROWS), BF16),
            pltpu.VMEM((3, ROWS, RANK_ROWS), BF16),
            pltpu.VMEM((3, RANK_ROWS, ROWS), BF16),
            pltpu.VMEM((RANK_ROWS, ROWS), F32),
            pltpu.VMEM((RANK_ROWS, ROWS), F32),
            pltpu.VMEM((TOKENS, SLICE), BF16),
            pltpu.VMEM((TOKENS, WIDTH), BF16),
            pltpu.VMEM((4, RANK_ROWS, SLICE), F32),
            pltpu.VMEM((RANK_ROWS, VALUE), F32),
            dma((6,)),
            dma((2,)),
            dma((CHUNKS,)),
            dma((CHUNKS,)),
            dma((CHUNKS,)),
            dma((CHUNKS,)),
            dma((2,)),
            dma((2,)),
            dma((2,)),
            dma((SLICES,)),
            dma((SLICES,)),
            dma((SLICES,)),
            dma((1,)),
        ],
        compiler_params=pltpu.CompilerParams(
            collective_id=0, has_side_effects=True, vmem_limit_bytes=60 * 2**20
        ),
        cost_estimate=pl.CostEstimate(flops=16 * 10**9, bytes_accessed=20 * 2**20, transcendentals=0),
        name="section_backward",
    )(
        acts[0],
        output_gradient[0],
        frozen[0],
        adapter_down.reshape(RANK_ROWS, WIDTH),
        adapter_up.reshape(RANK_ROWS, VALUE),
        assign,
        adapter_slot.reshape(1, -1),
    )
    return (
        passed[None],
        down_grad.reshape(1, 4, 64, WIDTH),
        up_grad.reshape(1, 4, 64, VALUE),
    )


def solution(mesh):
    tok = P("segment", "tok", None)
    mats = P("segment", "tok", None, None)
    return jax.shard_map(
        on_device,
        mesh=mesh,
        in_specs=(tok, tok, tok, mats, mats, P("segment", "tok"), P()),
        out_specs=(tok, mats, mats),
        check_vma=False,
    )
```

time: 349 us -> 201 us (0.58); the launches traced: 342 us -> 201 us
  waiting for transfers between devices: 191 us -> 0 us
  Pallas kernels: 0 us -> 188 us
  local copies, waits for them, and re-layouts: 65.8 us -> 11.8 us
  matrix products: 36.9 us -> 0 us
  starting transfers between devices: 32.3 us -> 0 us
  between operations: 14.2 us -> 0.64 us
    all_to_all x4 -> x0, waiting for transfers between devices: 190 us -> none  [the longest x1 99.8 us: on_device(): lax.all_to_all(adapter_rows.reshape(owner_ranks, slot_capacity, hidden_wi...]
    pallas_call x0 -> x1, Pallas kernels: none -> 188 us  [on_device(): pl.pallas_call(kernel, out_shape=(jax.ShapeDtypeStruct((TOKENS, WIDTH), B...]
    reshape x10 -> x0, local copies, waits for them, and re-layouts: 46.8 us -> none  [the longest x2 17.4 us: on_device(): recv_rows = recv_rows.reshape(slot_row_list, hidden_width)]
    dot_general x5 -> x0, matrix products: 36.9 us -> none  [the longest x1 12.7 us: on_device(): lax.dot_general(out_grads, lax.all_gather(frozen, 'tok', axis=1, tiled=Tr...]
    all_to_all x4 -> x0, starting transfers between devices: 29.5 us -> none  [the longest x1 12 us: on_device(): lax.all_to_all(send_rows.reshape(owner_ranks, slot_capacity, hidden_width...]
    unnamed x11 -> x5, local copies, waits for them, and re-layouts: 3.12 us -> 11.8 us
    scatter x3 -> x0, local copies, waits for them, and re-layouts: 8.38 us -> none  [the longest x1 6.52 us: on_device(): jnp.zeros((slot_row_list, hidden_width), jnp.bfloat16).at[target_owner]]
    gather x1 -> x0, local copies, waits for them, and re-layouts: 6.96 us -> none  [on_device(): returned_rows.reshape(slot_row_list, hidden_width)[target_owner]]
  transfers between devices with their start and end apart: 6 -> 0, of which waited for: 4 -> 0; matrix products, arithmetic and copies ran while one was open for 30% -> 0% of each run, Pallas kernels for 0% -> 0%
where the time goes in v1:
time: 201 us
  Pallas kernels  188 us (94%)
  local copies, waits for them, and re-layouts  11.8 us (6%)
    pallas_call x1, Pallas kernels, on_device(): pl.pallas_call(kernel, out_shape=(jax.ShapeDtypeStruct((TOKENS, WIDTH), B...  188 us
    unnamed x5, local copies, waits for them, and re-layouts  11.8 us

profile of v1, /device:TPU:1, one launch (start us, length us, event | category | flops | bytes accessed | tf_op | source)
XLA Modules:
  0.0 200.6 jit_solution(587360238464669154)
XLA Ops:
  0.6 188.1 %section_backward.1 = (bf16[128,8192]{1,0:T(8,128)(2,1)}, f32[256,8192]{1,0:T(8,128)}, f32[256,1024]{1,0:T(8,128)}) custom-call(bf16[128,8192]{1,0:T(8,128)(2,1)} %bitcast.13, bf16[128,1024]{1,0:T(8,128)(2,1)} %bitcast.16, bf16[256,1024]{1,0:T(8,128)(2,1)} %bitcast.14, bf16[256,8192]{1,0:T(8,128)(2,1)} %bitcast.12, bf16[256,1024]{1,0:T(8,128)(2,1)} %bitcast.15, ...), custom_call_target="tpu_custom_call" | custom-call | flops 16000000000 | bytes 20971520 | tf_op jit(solution)/shard_map/section_backward/pallas_call | solution.py:362
  188.8 3.1 %copy.13 = bf16[1,128,8192]{2,1,0:T(8,128)(2,1)} copy(bf16[1,128,8192]{2,1,0:T(8,128)(2,1)} %bitcast.10) | data formatting | bytes 4194304
  191.9 0.0 copy-start
  191.9 7.8 %copy.14 = f32[1,4,64,8192]{3,2,1,0:T(8,128)} copy(f32[1,4,64,8192]{3,2,1,0:T(8,128)} %bitcast.9) | data formatting | bytes 16777216
  199.7 0.0 copy-done
  199.7 1.0 copy.15
Async XLA Ops:
  191.9 7.8 %copy-start = (f32[256,1024]{1,0:T(8,128)S(1)}, f32[256,1024]{1,0:T(8,128)}, u32[]{:S(2)}) copy-start(f32[256,1024]{1,0:T(8,128)} %get-tuple-element.8) | copy-start | bytes 3145732

commit v2 on v1

--- a/solution.py
+++ b/solution.py
@@ -79,24 +79,24 @@
 def kernel(
     acts, grads, frozen, down, up, assign, slots,
     passed, down_grad, up_grad,
-    acts_v, grads_v, down_v, up_v, dest_row, dest_col,
-    gs, gr, fs, fr, rs, rr, gx, wy, ft, fp,
+    acts_v, down_v, up_v, dest_row, dest_col,
+    info, gs, gd, gr, fs, fr, rs, rr, gx, wy, ft, fp,
     lift_src, lift_t, mask_t, lift_q, liftt_q, low_q, low_t, pend, fin, dg, ug,
-    in_sem, g_sem, f_send, f_recv, r_send, r_recv, gx_sem, wy_sem, fp_sem, z_send, z_recv, dg_sem, ug_sem,
+    in_sem, info_sem, g_sem, f_send, f_recv, r_send, r_recv, gx_sem, wy_sem, fp_sem, z_send, z_recv, dg_sem, ug_sem,
 ):
     seg = lax.axis_index("segment")
     me = lax.axis_index("tok")
     y, x, core = me // 8, (me // 2) % 4, me % 2
     col8 = me % 8
     before, after = (seg + 3) % 4, (seg + 1) % 4
+    partner = y * 8 + x * 2 + (1 - core)
 
     loads = [
-        pltpu.make_async_copy(grads, grads_v, in_sem.at[0]),
+        pltpu.make_async_copy(grads, gx.at[col8], in_sem.at[0]),
         pltpu.make_async_copy(acts, acts_v, in_sem.at[1]),
         pltpu.make_async_copy(up, up_v, in_sem.at[2]),
         pltpu.make_async_copy(down, down_v, in_sem.at[3]),
         pltpu.make_async_copy(frozen, wy.at[y], in_sem.at[4]),
-        pltpu.make_async_copy(grads, gx.at[col8], in_sem.at[5]),
     ]
     for load in loads:
         load.start()
@@ -117,63 +117,76 @@
     earlier = one_hot(iota((TOKENS, TOKENS), 0) < iota((TOKENS, TOKENS), 1))
     rank = jnp.sum(hot * dot(hot.astype(BF16), earlier), axis=0, keepdims=True)
     dest = owner * CAP + rank.astype(jnp.int32)
-    dest_row[...] = jnp.broadcast_to(dest, (8, TOKENS))
+    dest_row[...] = jnp.where(iota((8, TOKENS), 0) == 0, dest, local)
+    info[col8] = dest_row[...]
     dest_col[...] = jnp.transpose(jnp.broadcast_to(dest.astype(F32), (TOKENS, TOKENS))).astype(jnp.int32)
-
-    local_hot = one_hot(local == iota((MARK, TOKENS), 0))
-    row = iota((ROWS, TOKENS), 0)
-    chosen = one_hot((dest == (row >> 4) * CAP + (row & 15)) & ((row & 15) < CAP))
-    gs[:, VALUE:] = dot_t(chosen, local_hot).astype(BF16)
-    loads[0].wait()
-    for c0 in range(0, VALUE, TILE):
-        gs[:, c0 : c0 + TILE] = dot(chosen, grads_v[:, c0 : c0 + TILE]).astype(BF16)
 
     def piece(owner_at):
         return pl.ds(pl.multiple_of(owner_at * PIECE, PIECE), PIECE)
 
-    def send_pieces(src, dst, send_sem, recv_sem):
-        def one(k, carry):
-            to = (me + k) % OWNERS
-            pltpu.make_async_remote_copy(
-                src_ref=src.at[piece(to)],
-                dst_ref=dst.at[piece(me)],
-                send_sem=send_sem,
-                recv_sem=recv_sem,
-                device_id=(seg, to),
-                device_id_type=MESH,
-            ).start()
+    def remote(src, dst, send_sem, recv_sem, to):
+        return pltpu.make_async_remote_copy(
+            src_ref=src, dst_ref=dst, send_sem=send_sem, recv_sem=recv_sem,
+            device_id=(seg, to), device_id_type=MESH,
+        )
+
+    def send_act(q, to):
+        remote(fs.at[q, piece(to)], fr.at[q, piece(me)], f_send.at[q], f_recv.at[q], to).start()
+
+    def send_term(q, to):
+        remote(rs.at[q, piece(to)], rr.at[q, piece(me)], r_send.at[q], r_recv.at[q], to).start()
+
+    def to_x(send, q, side):
+        for k in range(1, 4):
+            send(q, y * 8 + ((x + k) % 4) * 2 + side)
+
+    def to_y(send, q, side):
+        for k in range(1, 4):
+            send(q, ((y + k) % 4) * 8 + x * 2 + side)
+
+    def to_rest(send, q):
+        def one(n, carry):
+            ky, kx, side = n // 6 + 1, (n // 2) % 3 + 1, n % 2
+            send(q, ((y + ky) % 4) * 8 + ((x + kx) % 4) * 2 + side)
             return carry
 
-        lax.fori_loop(1, OWNERS, one, 0)
-        dst[piece(me)] = src[piece(me)]
+        lax.fori_loop(0, 18, one, 0)
+        send(q, partner)
 
     def wait_pieces(buf, sem):
         others = buf.at[pl.ds(0, ROWS - PIECE)]
         pltpu.make_async_copy(others, others, sem).wait()
 
+    def wait_blocks(buf, count, sem):
+        blocks = buf.at[pl.ds(0, count)]
+        pltpu.make_async_copy(blocks, blocks, sem).wait()
+
     pl.semaphore_wait(barrier, OWNERS)
-    send_pieces(gs, gr, g_sem.at[0], g_sem.at[1])
-
-    def send_frozen(k, carry):
-        to = ((y + k) % 4) * 8 + col8
-        pltpu.make_async_remote_copy(
-            src_ref=frozen, dst_ref=wy.at[y], send_sem=wy_sem.at[0], recv_sem=wy_sem.at[1],
-            device_id=(seg, to), device_id_type=MESH,
-        ).start()
-        return carry
-
-    def send_grads(k, carry):
-        to = y * 8 + (col8 + k) % 8
-        pltpu.make_async_remote_copy(
-            src_ref=grads, dst_ref=gx.at[col8], send_sem=gx_sem.at[0], recv_sem=gx_sem.at[1],
-            device_id=(seg, to), device_id_type=MESH,
-        ).start()
-        return carry
-
-    lax.fori_loop(1, 4, send_frozen, 0)
-    lax.fori_loop(1, 8, send_grads, 0)
-
-    def send_acts(q):
+
+    def send_info(k, carry):
+        remote(dest_row, info.at[col8], info_sem.at[0], info_sem.at[1], y * 8 + (col8 + k) % 8).start()
+        return carry
+
+    def send_frozen(part, carry):
+        at = piece(part)
+        for k in range(1, 4):
+            to = ((y + k) % 4) * 8 + col8
+            remote(frozen.at[at], wy.at[y, at], wy_sem.at[0], wy_sem.at[1], to).start()
+        return carry
+
+    def send_grads(part, carry):
+        at = piece(part)
+        for k in range(1, 4):
+            to = y * 8 + (col8 + 2 * k) % 8
+            remote(grads.at[at], gx.at[col8, at], gx_sem.at[0], gx_sem.at[1], to).start()
+        send_frozen(part, 0)
+        return carry
+
+    lax.fori_loop(1, 8, send_info, 0)
+    lax.fori_loop(0, TOKENS // PIECE, send_grads, 0)
+    remote(grads, gx.at[col8], gx_sem.at[2], gx_sem.at[3], partner).start()
+
+    def pack_acts(q):
         src = fs.at[q]
 
         def step(ct, carry):
@@ -187,28 +200,78 @@
             return carry
 
         lax.fori_loop(0, SLICE // TILE, step, 0)
-        send_pieces(src, fr.at[q], f_send.at[q], f_recv.at[q])
+        fr[q, piece(me)] = fs[q, piece(me)]
 
     loads[1].wait()
-    send_acts(0)
+    pack_acts(0)
+    to_rest(send_act, 0)
+    pack_acts(1)
+    wait_blocks(gx, 3, gx_sem.at[1])
+
+    def pass_grads(k, carry):
+        other = (col8 + 2 * k) % 8
+        remote(gx.at[other], gx.at[other], gx_sem.at[2], gx_sem.at[3], partner).start()
+        return carry
+
+    lax.fori_loop(1, 4, pass_grads, 0)
+    to_rest(send_act, 1)
+    pack_acts(2)
+
+    loads[0].wait()
+    wait_blocks(info, 7, info_sem.at[1])
+    wait_blocks(gx, 4, gx_sem.at[3])
+    dest_all = jnp.concatenate([info[k, 0:1] for k in range(8)], axis=1)
+    local_all = jnp.concatenate([info[k, 1:2] for k in range(8)], axis=1)
+    local_hot = one_hot(local_all == iota((MARK, 8 * TOKENS), 0))
+    wanted = (4 * 8 * CAP, 8 * TOKENS)
+    at_row = iota(wanted, 0)
+    target_y = (at_row >= 80).astype(jnp.int32) + (at_row >= 160).astype(jnp.int32) + (at_row >= 240).astype(jnp.int32)
+    within = at_row - 80 * target_y
+    source = (within * 205) >> 11
+    spot = (target_y * 8 + col8) * CAP + within - CAP * source
+    chosen = one_hot((dest_all == spot) & (source == (iota(wanted, 1) >> 7)))
+    gs[:, :, VALUE:] = dot_t(chosen, local_hot).astype(BF16).reshape(4, 8 * CAP, MARK)
+    for c0 in range(0, VALUE, TILE):
+        part = gx[:, :, c0 : c0 + TILE].reshape(8 * TOKENS, TILE)
+        gs[:, :, c0 : c0 + TILE] = dot(chosen, part).astype(BF16).reshape(4, 8 * CAP, TILE)
+    gd[y] = gs[y]
+
+    def send_rows(part, carry):
+        at = piece(part)
+        for k in range(1, 4):
+            other = (y + k) % 4
+            remote(gs.at[other, at], gd.at[y, at], g_sem.at[0], g_sem.at[1], other * 8 + col8).start()
+        to_x(send_act, part // 2, part % 2)
+        return carry
+
+    lax.fori_loop(0, 8 * CAP // PIECE, send_rows, 0)
+    to_x(send_act, 2, 1)
+    to_rest(send_act, 2)
+    pack_acts(3)
+    to_rest(send_act, 3)
+    pack_acts(4)
 
     loads[2].wait()
-    wait_pieces(gr, g_sem.at[1])
+    wait_blocks(gd, 3, g_sem.at[1])
+    row, col = iota((8 * PIECE, 8 * CAP), 0), iota((8 * PIECE, 8 * CAP), 1)
+    place = one_hot((col == (row >> 4) * CAP + (row & 15)) & ((row & 15) < CAP))
+    for yy in range(4):
+        gr[yy * 128 : yy * 128 + 128] = dot(place, gd[yy]).astype(BF16)
     expand = one_hot(iota((RANK_ROWS, MARK), 0) >> 6 == iota((RANK_ROWS, MARK), 1))
     marks = gr[:, VALUE:]
-    mask_t[...] = dot_t(expand, marks).astype(BF16)
-    lift_src[...] = (ADAPTER_SCALE * dot_t(gr[:, :VALUE], up_v[...]) * dot_t(marks, expand)).astype(BF16)
-    lift_t[...] = jnp.transpose(lift_src[...].astype(F32)).astype(BF16)
+    lifted = (ADAPTER_SCALE * dot_t(gr[:, :VALUE], up_v[...]) * dot_t(marks, expand)).astype(BF16)
+    for b in range(4):
+        lift_src[:, b * RANK_ROWS : (b + 1) * RANK_ROWS] = lifted[b * 128 : b * 128 + 128]
 
     loads[3].wait()
 
-    def send_terms(q):
+    def make_terms(q):
         dst = rs.at[q]
         js = slices_of(q)
         for n, j in enumerate(js):
-            move = spread(q, [j], 0).astype(BF16)
-            for b in range(0, ROWS, 128):
-                lift_q[n, b : b + 128] = dot(move, lift_src[b : b + 128]).astype(BF16)
+            moved = dot(spread(q, [j], 0).astype(BF16), lift_src[...]).astype(BF16)
+            for b in range(4):
+                lift_q[n, b * 128 : b * 128 + 128] = moved[:, b * RANK_ROWS : (b + 1) * RANK_ROWS]
 
         def step(ct, carry):
             cols = pl.ds(pl.multiple_of(ct * TILE, TILE), TILE)
@@ -221,15 +284,29 @@
             return carry
 
         lax.fori_loop(0, SLICE // TILE, step, 0)
-        send_pieces(dst, rr.at[q], r_send.at[q], r_recv.at[q])
-
-    send_terms(0)
-    send_terms(1)
+        rr[q, piece(me)] = rs[q, piece(me)]
+
+    make_terms(0)
+    make_terms(1)
+
+    def send_frozen_acts(n, carry):
+        send_frozen(8 + n, 0)
+        to_x(send_act, 3 + n // 2, n % 2)
+        return carry
+
+    def send_frozen_terms(n, carry):
+        send_frozen(12 + n, 0)
+        to_x(send_term, n // 2, n % 2)
+        return carry
+
+    lax.fori_loop(0, 4, send_frozen_acts, 0)
+    lax.fori_loop(0, 4, send_frozen_terms, 0)
+    to_rest(send_term, 0)
+    to_rest(send_term, 1)
+    make_terms(2)
 
     loads[4].wait()
-    loads[5].wait()
-    pltpu.make_async_copy(wy.at[pl.ds(0, 3)], wy.at[pl.ds(0, 3)], wy_sem.at[1]).wait()
-    pltpu.make_async_copy(gx.at[pl.ds(0, 7)], gx.at[pl.ds(0, 7)], gx_sem.at[1]).wait()
+    wait_blocks(wy, 3, wy_sem.at[1])
 
     def frozen_step(k, carry):
         half, yy = k // 4, k % 4
@@ -241,22 +318,51 @@
     lax.fori_loop(0, 8, frozen_step, 0)
     fp[col8] = ft[col8]
 
-    def send_tiles(k, carry):
-        other = (col8 + k) % 8
-        pltpu.make_async_remote_copy(
-            src_ref=ft.at[other], dst_ref=fp.at[col8], send_sem=fp_sem.at[0], recv_sem=fp_sem.at[1],
-            device_id=(seg, y * 8 + other), device_id_type=MESH,
-        ).start()
-        return carry
-
-    lax.fori_loop(1, 8, send_tiles, 0)
-
-    for q in range(2, CHUNKS):
-        send_terms(q)
-    for q in range(1, CHUNKS):
-        send_acts(q)
+    def send_tiles(part):
+        at = piece(part)
+        for k in range(1, 8):
+            other = (col8 + k) % 8
+            remote(ft.at[other, at], fp.at[col8, at], fp_sem.at[0], fp_sem.at[1], y * 8 + other).start()
+
+    def send_tiles_acts(n, carry):
+        send_tiles(n)
+        to_y(send_act, n, 0)
+        to_y(send_act, n, 1)
+        return carry
+
+    def send_tiles_terms(n, carry):
+        send_tiles(CHUNKS + n)
+        to_y(send_term, n, 0)
+        to_y(send_term, n, 1)
+        return carry
+
+    lax.fori_loop(0, CHUNKS, send_tiles_acts, 0)
+    lax.fori_loop(0, TOKENS // PIECE - CHUNKS, send_tiles_terms, 0)
+
+    def send_lines(q, carry):
+        to_x(send_term, q, 0)
+        to_x(send_term, q, 1)
+        return carry
+
+    def send_columns(q, carry):
+        to_y(send_term, q, 0)
+        to_y(send_term, q, 1)
+        return carry
+
+    send_lines(2, 0)
+    to_rest(send_term, 2)
+    for q in range(3, CHUNKS):
+        make_terms(q)
+        send_lines(q, 0)
+        send_columns(q, 0)
+        to_rest(send_term, q)
+    to_rest(send_act, 4)
 
     low_t[...] = jnp.zeros_like(low_t)
+    mask_t[...] = dot_t(expand, gr[:, VALUE:]).astype(BF16)
+    for b in range(4):
+        block = lift_src[:, b * RANK_ROWS : (b + 1) * RANK_ROWS].astype(F32)
+        lift_t[:, b * 128 : b * 128 + 128] = jnp.transpose(block).astype(BF16)
 
     def out_copy(j):
         cols = pl.ds(j * SLICE, SLICE)
@@ -328,12 +434,17 @@
             if last_chunk(j) == q:
                 hand_on(j).start()
 
+    wait_blocks(fp, 7, fp_sem.at[1])
+    take_terms(0)
+    take_terms(1)
     take_acts(0)
-    pltpu.make_async_copy(fp.at[pl.ds(0, 7)], fp.at[pl.ds(0, 7)], fp_sem.at[1]).wait()
-    for q in range(CHUNKS):
-        take_terms(q)
-    for q in range(1, CHUNKS):
-        take_acts(q)
+    take_terms(2)
+    take_acts(1)
+    take_terms(3)
+    take_acts(2)
+    take_acts(3)
+    take_terms(4)
+    take_acts(4)
 
     low_b = (low_t[...] * mask_t[...].astype(F32)).astype(BF16)
     for c0 in range(0, VALUE, TILE):
@@ -341,10 +452,12 @@
     up_copy = pltpu.make_async_copy(ug, up_grad, ug_sem.at[0])
     up_copy.start()
 
-    wait_pieces(gs, g_sem.at[0])
-    pltpu.make_async_copy(wy.at[pl.ds(0, 3)], wy.at[pl.ds(0, 3)], wy_sem.at[0]).wait()
-    pltpu.make_async_copy(gx.at[pl.ds(0, 7)], gx.at[pl.ds(0, 7)], gx_sem.at[0]).wait()
-    pltpu.make_async_copy(ft.at[pl.ds(0, 7)], ft.at[pl.ds(0, 7)], fp_sem.at[0]).wait()
+    wait_blocks(info, 7, info_sem.at[0])
+    wait_blocks(gs, 3, g_sem.at[0])
+    wait_blocks(wy, 3, wy_sem.at[0])
+    wait_blocks(gx, 3, gx_sem.at[0])
+    wait_blocks(gx, 4, gx_sem.at[2])
+    wait_blocks(ft, 7, fp_sem.at[0])
     for q in range(CHUNKS):
         wait_pieces(fs.at[q], f_send.at[q])
         wait_pieces(rs.at[q], r_send.at[q])
@@ -370,12 +483,13 @@
         out_specs=[hbm] * 3,
         scratch_shapes=[
             pltpu.VMEM((TOKENS, WIDTH), BF16),
-            pltpu.VMEM((TOKENS, VALUE), BF16),
             pltpu.VMEM((RANK_ROWS, WIDTH), BF16),
             pltpu.VMEM((RANK_ROWS, VALUE), BF16),
             pltpu.VMEM((8, TOKENS), jnp.int32),
             pltpu.VMEM((TOKENS, TOKENS), jnp.int32),
-            pltpu.VMEM((ROWS, VALUE + MARK), BF16),
+            pltpu.VMEM((8, 8, TOKENS), jnp.int32),
+            pltpu.VMEM((4, 8 * CAP, VALUE + MARK), BF16),
+            pltpu.VMEM((4, 8 * CAP, VALUE + MARK), BF16),
             pltpu.VMEM((ROWS, VALUE + MARK), BF16),
             pltpu.VMEM((CHUNKS, ROWS, SLICE), BF16),
             pltpu.VMEM((CHUNKS, ROWS, SLICE), BF16),
@@ -385,7 +499,7 @@
             pltpu.VMEM((4, 256, VALUE), BF16),
             pltpu.VMEM((8, TOKENS, 1024), BF16),
             pltpu.VMEM((8, TOKENS, 1024), BF16),
-            pltpu.VMEM((ROWS, RANK_ROWS), BF16),
+            pltpu.VMEM((128, 4 * RANK_ROWS), BF16),
             pltpu.VMEM((RANK_ROWS, ROWS), BF16),
             pltpu.VMEM((RANK_ROWS, ROWS), BF16),
             pltpu.VMEM((3, ROWS, RANK_ROWS), BF16),
@@ -396,13 +510,14 @@
             pltpu.VMEM((TOKENS, WIDTH), BF16),
             pltpu.VMEM((4, RANK_ROWS, SLICE), F32),
             pltpu.VMEM((RANK_ROWS, VALUE), F32),
-            dma((6,)),
+            dma((5,)),
+            dma((2,)),
             dma((2,)),
             dma((CHUNKS,)),
             dma((CHUNKS,)),
             dma((CHUNKS,)),
             dma((CHUNKS,)),
-            dma((2,)),
+            dma((4,)),
             dma((2,)),
             dma((2,)),
             dma((SLICES,)),

time: 201 us -> 187 us (0.930); the launches traced: 201 us -> 184 us
  Pallas kernels: 188 us -> 172 us
    pallas_call x1, Pallas kernels: 188 us -> 172 us  [on_device(): pl.pallas_call(kernel, out_shape=(jax.ShapeDtypeStruct((TOKENS, WIDTH), B...]
where the time goes in v2:
time: 187 us; the launch traced here: 184 us
  Pallas kernels  172 us (92%)
  local copies, waits for them, and re-layouts  11.8 us (6%)
    pallas_call x1, Pallas kernels, on_device(): pl.pallas_call(kernel, out_shape=(jax.ShapeDtypeStruct((TOKENS, WIDTH), B...  172 us
    unnamed x5, local copies, waits for them, and re-layouts  11.8 us

profile of v2, /device:TPU:1, one launch (start us, length us, event | category | flops | bytes accessed | tf_op | source)
XLA Modules:
  0.0 184.5 jit_solution(16720345576134625893)
XLA Ops:
  0.6 172.0 %section_backward.1 = (bf16[128,8192]{1,0:T(8,128)(2,1)}, f32[256,8192]{1,0:T(8,128)}, f32[256,1024]{1,0:T(8,128)}) custom-call(bf16[128,8192]{1,0:T(8,128)(2,1)} %bitcast.13, bf16[128,1024]{1,0:T(8,128)(2,1)} %bitcast.16, bf16[256,1024]{1,0:T(8,128)(2,1)} %bitcast.14, bf16[256,8192]{1,0:T(8,128)(2,1)} %bitcast.12, bf16[256,1024]{1,0:T(8,128)(2,1)} %bitcast.15, ...), custom_call_target="tpu_custom_call" | custom-call | flops 16000000000 | bytes 20971520 | tf_op jit(solution)/shard_map/section_backward/pallas_call | solution.py:475
  172.6 3.1 %copy.13 = bf16[1,128,8192]{2,1,0:T(8,128)(2,1)} copy(bf16[1,128,8192]{2,1,0:T(8,128)(2,1)} %bitcast.10) | data formatting | bytes 4194304
  175.7 0.0 copy-start
  175.7 7.8 %copy.14 = f32[1,4,64,8192]{3,2,1,0:T(8,128)} copy(f32[1,4,64,8192]{3,2,1,0:T(8,128)} %bitcast.9) | data formatting | bytes 16777216
  183.5 0.0 copy-done
  183.5 1.0 copy.15
Async XLA Ops:
  175.7 7.8 %copy-start = (f32[256,1024]{1,0:T(8,128)S(1)}, f32[256,1024]{1,0:T(8,128)}, u32[]{:S(2)}) copy-start(f32[256,1024]{1,0:T(8,128)} %get-tuple-element.8) | copy-start | bytes 3145732

commit v3 on v2

--- a/solution.py
+++ b/solution.py
@@ -251,6 +251,13 @@
     to_rest(send_act, 3)
     pack_acts(4)
 
+    def send_frozen_acts(n, carry):
+        send_frozen(8 + n, 0)
+        to_x(send_act, 3 + n // 2, n % 2)
+        return carry
+
+    lax.fori_loop(0, 4, send_frozen_acts, 0)
+
     loads[2].wait()
     wait_blocks(gd, 3, g_sem.at[1])
     row, col = iota((8 * PIECE, 8 * CAP), 0), iota((8 * PIECE, 8 * CAP), 1)
@@ -289,17 +296,11 @@
     make_terms(0)
     make_terms(1)
 
-    def send_frozen_acts(n, carry):
-        send_frozen(8 + n, 0)
-        to_x(send_act, 3 + n // 2, n % 2)
-        return carry
-
     def send_frozen_terms(n, carry):
         send_frozen(12 + n, 0)
         to_x(send_term, n // 2, n % 2)
         return carry
 
-    lax.fori_loop(0, 4, send_frozen_acts, 0)
     lax.fori_loop(0, 4, send_frozen_terms, 0)
     to_rest(send_term, 0)
     to_rest(send_term, 1)
@@ -466,6 +467,26 @@
     for j in range(SLICES - 4, SLICES):
         out_copy(j).wait()
     up_copy.wait()
+
+
+def settle(passed, down_grad, up_grad, passed_out, down_out, up_out, p_v, d_v, u_v, sem, sem_out):
+    moves = []
+    for src, mid, dst, rows in (
+        (down_grad, d_v, down_out, 32), (passed, p_v, passed_out, 64), (up_grad, u_v, up_out, 256),
+    ):
+        for r0 in range(0, src.shape[0], rows):
+            at, n = pl.ds(r0, rows), len(moves)
+            moves.append((
+                pltpu.make_async_copy(src.at[at], mid.at[at], sem.at[n]),
+                pltpu.make_async_copy(mid.at[at], dst.at[at], sem_out.at[n]),
+            ))
+    for load, _ in moves:
+        load.start()
+    for load, store in moves:
+        load.wait()
+        store.start()
+    for _, store in moves:
+        store.wait()
 
 
 def on_device(acts, output_gradient, frozen, adapter_down, adapter_up, assign, adapter_slot):
@@ -539,6 +560,25 @@
         assign,
         adapter_slot.reshape(1, -1),
     )
+    passed, down_grad, up_grad = pl.pallas_call(
+        settle,
+        out_shape=(
+            jax.ShapeDtypeStruct((TOKENS, WIDTH), BF16),
+            jax.ShapeDtypeStruct((RANK_ROWS, WIDTH), F32),
+            jax.ShapeDtypeStruct((RANK_ROWS, VALUE), F32),
+        ),
+        in_specs=[hbm] * 3,
+        out_specs=[hbm] * 3,
+        scratch_shapes=[
+            pltpu.VMEM((TOKENS, WIDTH), BF16),
+            pltpu.VMEM((RANK_ROWS, WIDTH), F32),
+            pltpu.VMEM((RANK_ROWS, VALUE), F32),
+            dma((11,)),
+            dma((11,)),
+        ],
+        compiler_params=pltpu.CompilerParams(vmem_limit_bytes=60 * 2**20),
+        name="settle",
+    )(passed, down_grad, up_grad)
     return (
         passed[None],
         down_grad.reshape(1, 4, 64, WIDTH),

time: 187 us -> 179 us (0.957); the launches traced: 184 us -> 179 us
  local copies, waits for them, and re-layouts: 11.8 us -> 0 us
  Pallas kernels: 172 us -> 178 us
    unnamed x5 -> x0, local copies, waits for them, and re-layouts: 11.8 us -> none
    pallas_call x0 -> x1, Pallas kernels: none -> 8.84 us  [on_device(): pl.pallas_call(settle, out_shape=(jax.ShapeDtypeStruct((TOKENS, WIDTH), B...]
    pallas_call x1, Pallas kernels: 172 us -> 169 us  [on_device(): pl.pallas_call(kernel, out_shape=(jax.ShapeDtypeStruct((TOKENS, WIDTH), B...]
where the time goes in v3:
time: 179 us
  Pallas kernels  178 us (99%)
    pallas_call x1, Pallas kernels, on_device(): pl.pallas_call(kernel, out_shape=(jax.ShapeDtypeStruct((TOKENS, WIDTH), B...  169 us
    pallas_call x1, Pallas kernels, on_device(): pl.pallas_call(settle, out_shape=(jax.ShapeDtypeStruct((TOKENS, WIDTH), B...  8.84 us

profile of v3, /device:TPU:1, one launch (start us, length us, event | category | flops | bytes accessed | tf_op | source)
XLA Modules:
  0.0 178.9 jit_solution(17051728328373425193)
XLA Ops:
  0.6 169.3 %section_backward.1 = (bf16[128,8192]{1,0:T(8,128)(2,1)}, f32[256,8192]{1,0:T(8,128)}, f32[256,1024]{1,0:T(8,128)}) custom-call(bf16[128,8192]{1,0:T(8,128)(2,1)} %bitcast.11, bf16[128,1024]{1,0:T(8,128)(2,1)} %bitcast.16, bf16[256,1024]{1,0:T(8,128)(2,1)} %bitcast.14, bf16[256,8192]{1,0:T(8,128)(2,1)} %bitcast.10, bf16[256,1024]{1,0:T(8,128)(2,1)} %bitcast.15, ...), custom_call_target="tpu_custom_call" | custom-call | flops 16000000000 | bytes 20971520 | tf_op jit(solution)/shard_map/section_backward/pallas_call | solution.py:496
  169.9 8.8 %settle.1 = (bf16[128,8192]{1,0:T(8,128)(2,1)}, f32[256,8192]{1,0:T(8,128)}, f32[256,1024]{1,0:T(8,128)}) custom-call(bf16[128,8192]{1,0:T(8,128)(2,1)} %get-tuple-element.9.passed, f32[256,8192]{1,0:T(8,128)} %get-tuple-element.10.down_grad, f32[256,1024]{1,0:T(8,128)} %get-tuple-element.11.up_grad), custom_call_target="tpu_custom_call" | custom-call | tf_op jit(solution)/shard_map/settle/pallas_call | solution.py:563
